TPU v7x, 32 devices: a whole 2x2x4 slice. The times are simulated.
32 devices in a mesh: group: 2 (over x), tm: 16 (over z, y, core).
Axes of the slice: x: 2, y: 2, z: 4, core: 2. Of those that a mesh axis runs over, the one named last changes fastest.
Arguments:
- queries: bfloat16 [8192, 1536], P(('group', 'tm')), parts along dimension 0, may hold values from -7 to 7, as said below
- keys: bfloat16 [8192, 1536], P(('group', 'tm')), parts along dimension 0, may hold values from -6 to 6, as said below
- values: bfloat16 [8192, 1536], P(('group', 'tm')), parts along dimension 0, may hold values from -6 to 6
- grad_out: bfloat16 [8192, 1536], P(('group', 'tm')), parts along dimension 0, may hold values from -96 to 96
- block_list: int32 [128, 30], P(('group', 'tm')), parts along dimension 0, may hold values 0 or 1
Outputs:
- grad_queries: bfloat16 [8192, 1536], P(('group', 'tm')), parts along dimension 0
- grad_keys: bfloat16 [8192, 1536], P(('group', 'tm')), parts along dimension 0
- grad_values: bfloat16 [8192, 1536], P(('group', 'tm')), parts along dimension 0
There are 2 independent parts, one for each index of `group`. A program takes and returns all parts, laid end to end along the dimension named above; each array names one. Nothing has to cross between parts.
Inputs may be any that keep to these rules, and one draw needn't show every extreme that they name: `queries`: entries of order one. `keys`: entries of order one. `block_list`: columns follow the candidate order of the steps.
All inputs are finite; a program needn't handle non-finite values. No bound on the sum of `block_list` on one device may be relied on, other than what follows from the above.
Results may differ from a plain program's by a relative error of at most 0.0073.
Values may be sent and summed in bfloat16 or wider, within the bound.
A program may use at most 128 MiB of HBM per device.

v0:
```python
import jax
import jax.numpy as jnp
import numpy as np
from jax import lax
from jax.sharding import PartitionSpec as P

HEADS = 12
HDIM = 128
BLOCK = 64
REACH = 2
FRAMES = 2
BANDS = 2


def from_behind(value, axis, steps):
    count = lax.axis_size(axis)
    first, last = (max(0, -steps), min(count, count - steps))
    return lax.ppermute(value, axis, [(source, source + steps) for source in range(first, last)])


def settle(tensor):
    return lax.optimization_barrier(tensor.astype(jnp.bfloat16)).astype(jnp.float32)


def pair_tables(slots):
    blocks_group = FRAMES * BANDS
    query_block = np.arange(blocks_group)[:, None]
    key_block = np.arange(slots * blocks_group)[None, :]
    slot_of = key_block // blocks_group
    frame_key = key_block // BANDS % FRAMES
    band_key = key_block % BANDS
    frame_query = query_block // BANDS
    band_query = query_block % BANDS
    cand = (slot_of * FRAMES + frame_key) * 3 + band_key - band_query + 1
    own_block = (slot_of == REACH) & (frame_key == frame_query) & (band_key == band_query)
    cand = cand + 0 * query_block
    slot_full = slot_of + 0 * query_block
    return (cand, own_block, slot_full)


def listed_mask(block_rows, group_index, groups):
    slots = 2 * REACH + 1
    cand, own_block, slot_full = pair_tables(slots)
    chosen = (block_rows > 0)[np.arange(FRAMES * BANDS)[:, None], cand]
    group_pos = group_index + jnp.asarray(slot_full, jnp.int32) - REACH
    group_ok = (group_pos >= 0) & (group_pos < groups)
    allowed = chosen & group_ok | jnp.asarray(own_block)
    return allowed[:, None, :, None]


def group_grads(query_rows, grad_rows, key_window, value_window, block_rows, group_index, groups):
    scaling = HDIM ** (-0.5)
    allowed = listed_mask(block_rows, group_index, groups)
    slots = key_window.shape[0]
    tok_dev = query_rows.shape[0]
    width = query_rows.shape[1]
    key_flat = key_window.reshape(slots * tok_dev, width)
    value_flat = value_window.reshape(slots * tok_dev, width)
    query_list, key_list, value_list, log_list, delta_list = ([], [], [], [], [])
    for head_index in range(HEADS):
        cols = slice(head_index * HDIM, (head_index + 1) * HDIM)
        query_head = query_rows[:, cols]
        grad_head = grad_rows[:, cols]
        key_head = key_flat[:, cols]
        value_head = value_flat[:, cols]
        scores = (
            jnp.einsum("qd,kd->qk", query_head, key_head, preferred_element_type=jnp.float32)
            * scaling
        )
        shaped = jnp.where(
            allowed, scores.reshape(FRAMES * BANDS, BLOCK, slots * FRAMES * BANDS, BLOCK), -jnp.inf
        )
        row_max = jnp.max(shaped, axis=(2, 3), keepdims=True)
        log_total = row_max + jnp.log(
            jnp.sum(jnp.exp(shaped - row_max), axis=(2, 3), keepdims=True)
        )
        weights = jnp.exp(shaped - log_total).reshape(scores.shape)
        weights_low = weights.astype(jnp.bfloat16)
        attended = jnp.einsum(
            "qk,kd->qd", weights_low, value_head, preferred_element_type=jnp.float32
        )
        deltas = jnp.sum(grad_head.astype(jnp.float32) * attended, axis=-1, keepdims=True)
        grad_probs = jnp.einsum(
            "qd,kd->qk", grad_head, value_head, preferred_element_type=jnp.float32
        )
        grad_scores = (weights * (grad_probs - deltas)).astype(jnp.bfloat16)
        query_list.append(
            jnp.einsum("qk,kd->qd", grad_scores, key_head, preferred_element_type=jnp.float32)
            * scaling
        )
        log_list.append(log_total.reshape(tok_dev))
        delta_list.append(deltas.reshape(tok_dev))
        key_grad = (
            jnp.einsum("qk,qd->kd", grad_scores, query_head, preferred_element_type=jnp.float32)
            * scaling
        )
        value_grad = jnp.einsum(
            "qk,qd->kd", weights_low, grad_head, preferred_element_type=jnp.float32
        )
        key_list.append(key_grad.reshape(slots, tok_dev, HDIM))
        value_list.append(value_grad.reshape(slots, tok_dev, HDIM))
    key_all = jnp.concatenate(key_list, axis=-1)
    value_all = jnp.concatenate(value_list, axis=-1)
    return (
        jnp.concatenate(query_list, axis=-1),
        key_all,
        value_all,
        jnp.stack(log_list),
        jnp.stack(delta_list),
    )


def local(queries, keys, values, grad_out, block_list):
    groups = lax.axis_size("tm")
    here_index = lax.axis_index("tm")
    key_parts = []
    value_parts = []
    for offset in range(-REACH, REACH + 1):
        if offset == 0:
            key_parts.append(keys)
            value_parts.append(values)
        else:
            near_keys, near_values = from_behind((keys, values), "tm", -offset)
            key_parts.append(near_keys)
            value_parts.append(near_values)
    key_window = jnp.stack(key_parts)
    value_window = jnp.stack(value_parts)
    key_total = jnp.zeros(keys.shape, jnp.float32)
    value_total = jnp.zeros(values.shape, jnp.float32)
    query_grad, key_grad, value_grad, log_totals, deltas = group_grads(
        queries, grad_out, key_window, value_window, block_list, here_index, groups
    )
    for offset in range(-REACH, REACH + 1):
        slot_index = offset + REACH
        if offset == 0:
            key_total = key_total + settle(key_grad[slot_index])
            value_total = value_total + settle(value_grad[slot_index])
        else:
            back_keys, back_values = from_behind(
                (
                    key_grad[slot_index].astype(jnp.bfloat16),
                    value_grad[slot_index].astype(jnp.bfloat16),
                ),
                "tm",
                offset,
            )
            key_total = key_total + back_keys.astype(jnp.float32)
            value_total = value_total + back_values.astype(jnp.float32)
    return (
        query_grad.astype(jnp.bfloat16),
        key_total.astype(jnp.bfloat16),
        value_total.astype(jnp.bfloat16),
    )


def solution(mesh):
    placed = (
        P(("group", "tm"), None),
        P(("group", "tm"), None),
        P(("group", "tm"), None),
        P(("group", "tm"), None),
        P(("group", "tm"), None),
    )
    return jax.shard_map(
        local,
        mesh=mesh,
        in_specs=placed,
        out_specs=(P(("group", "tm"), None), P(("group", "tm"), None), P(("group", "tm"), None)),
        check_vma=False,
    )
```

profile of v0, /device:TPU:16, one launch (start us, length us, event | category | flops | bytes accessed | tf_op | source)
XLA Modules:
  0.0 256.1 jit_solution(282285221689418240)
XLA Ops:
  0.6 3.6 %collective-permute-start = (bf16[256,1536]{1,0:T(8,128)(2,1)}, bf16[256,1536]{1,0:T(8,128)(2,1)}, u32[]{:S(2)}, u32[]{:S(2)}) collective-permute-start(bf16[256,1536]{1,0:T(8,128)(2,1)} %param.12), channel_id=1, source_target_pairs={{0,2},{1,3},{2,4},{3,5},{4,6},{5,7},{6,8},{7,9},{8,10},{9,11},{10,... | collective-permute-start | bytes 2359304 | tf_op jit(solution)/shard_map/ppermute | solution.py:18
  4.2 1.9 collective-permute-start.1
  6.1 4.5 %collective-permute-start.2 = (bf16[256,1536]{1,0:T(8,128)(2,1)}, bf16[256,1536]{1,0:T(8,128)(2,1)}, u32[]{:S(2)}, u32[]{:S(2)}) collective-permute-start(bf16[256,1536]{1,0:T(8,128)(2,1)} %param.12), channel_id=1, source_target_pairs={{1,0},{2,1},{3,2},{4,3},{5,4},{6,5},{7,6},{8,7},{9,8},{10,9},{11,1... | collective-permute-start | bytes 2359304 | tf_op jit(solution)/shard_map/ppermute | solution.py:18
  10.7 2.4 collective-permute-start.3
  13.1 3.4 %collective-permute-start.4 = (bf16[256,1536]{1,0:T(8,128)(2,1)}, bf16[256,1536]{1,0:T(8,128)(2,1)S(1)}, u32[]{:S(2)}, u32[]{:S(2)}) collective-permute-start(bf16[256,1536]{1,0:T(8,128)(2,1)} %param.13), channel_id=1, source_target_pairs={{0,2},{1,3},{2,4},{3,5},{4,6},{5,7},{6,8},{7,9},{8,10},{9,11},{10,... | collective-permute-start | bytes 2359304 | tf_op jit(solution)/shard_map/ppermute | solution.py:18
  17.2 2.1 gather_fusion
  20.7 1.1 broadcast_in_dim.106
  22.7 1.6 copy.44
  24.2 1.6 copy.45
  25.8 1.6 copy.46
  27.3 1.6 copy.47
  28.9 1.6 copy.48
  30.5 1.6 copy.49
  32.0 1.6 copy.50
  33.6 1.6 copy.51
  35.1 1.6 copy.52
  36.7 1.6 copy.53
  38.3 1.6 copy.54
  40.6 7.1 %collective-permute-done = bf16[256,1536]{1,0:T(8,128)(2,1)} collective-permute-done((bf16[256,1536]{1,0:T(8,128)(2,1)}, bf16[256,1536]{1,0:T(8,128)(2,1)}, u32[]{:S(2)}, u32[]{:S(2)}) %collective-permute-start) | collective-permute-done | bytes 786464 | tf_op jit(solution)/shard_map/ppermute | solution.py:18
  47.7 1.9 collective-permute-start.5
  49.6 1.2 bitcast_dynamic-update-slice_fusion.9
  50.8 4.5 %collective-permute-start.6 = (bf16[256,1536]{1,0:T(8,128)(2,1)S(1)}, bf16[256,1536]{1,0:T(8,128)(2,1)S(1)}, u32[]{:S(2)}, u32[]{:S(2)}) collective-permute-start(bf16[256,1536]{1,0:T(8,128)(2,1)S(1)} %copy-done.3), channel_id=1, source_target_pairs={{1,0},{2,1},{3,2},{4,3},{5,4},{6,5},{7,6},{8,7},{9,8},{10,9},{11,1... | collective-permute-start | bytes 2359304 | tf_op jit(solution)/shard_map/ppermute | solution.py:18
  55.4 1.2 bitcast_dynamic-update-slice_fusion.8
  56.7 21.8 %collective-permute-start.7 = (bf16[256,1536]{1,0:T(8,128)(2,1)S(1)}, bf16[256,1536]{1,0:T(8,128)(2,1)S(1)}, u32[]{:S(2)}, u32[]{:S(2)}) collective-permute-start(bf16[256,1536]{1,0:T(8,128)(2,1)S(1)} %copy-done.3), channel_id=1, source_target_pairs={{2,0},{3,1},{4,2},{5,3},{6,4},{7,5},{8,6},{9,7},{10,8},{11,9},{12,... | collective-permute-start | bytes 2359304 | tf_op jit(solution)/shard_map/ppermute | solution.py:18
  78.5 1.2 bitcast_dynamic-update-slice_fusion.6
  79.7 4.5 %collective-permute-done.3 = bf16[256,1536]{1,0:T(8,128)(2,1)S(1)} collective-permute-done((bf16[256,1536]{1,0:T(8,128)(2,1)}, bf16[256,1536]{1,0:T(8,128)(2,1)S(1)}, u32[]{:S(2)}, u32[]{:S(2)}) %collective-permute-start.3) | collective-permute-done | bytes 786464 | tf_op jit(solution)/shard_map/ppermute | solution.py:18
  90.0 17.3 %collective-permute-done.7 = bf16[256,1536]{1,0:T(8,128)(2,1)S(1)} collective-permute-done((bf16[256,1536]{1,0:T(8,128)(2,1)S(1)}, bf16[256,1536]{1,0:T(8,128)(2,1)S(1)}, u32[]{:S(2)}, u32[]{:S(2)}) %collective-permute-start.7) | collective-permute-done | bytes 786464 | tf_op jit(solution)/shard_map/ppermute | solution.py:18
  111.5 1.0 fusion.75
  114.5 1.0 fusion.77
  117.6 1.0 fusion.79
  120.7 1.0 fusion.81
  139.6 1.8 slice_bitcast_fusion.9
  146.4 4.3 %collective-permute-start.15 = (bf16[256,1536]{0,1:T(8,128)(2,1)S(1)}, bf16[256,1536]{0,1:T(8,128)(2,1)}, u32[]{:S(2)}, u32[]{:S(2)}) collective-permute-start(bf16[256,1536]{0,1:T(8,128)(2,1)S(1)} %get-tuple-element.13), channel_id=1, source_target_pairs={{0,2},{1,3},{2,4},{3,5},{4,6},{5,7},{6,8},{7,9},{8,10},{9,11},{10,... | collective-permute-start | bytes 2359304 | tf_op jit(solution)/shard_map/ppermute | solution.py:18
  150.7 1.9 collective-permute-start.14
  152.7 4.5 %collective-permute-start.13 = (bf16[256,1536]{0,1:T(8,128)(2,1)S(1)}, bf16[256,1536]{0,1:T(8,128)(2,1)}, u32[]{:S(2)}, u32[]{:S(2)}) collective-permute-start(bf16[256,1536]{0,1:T(8,128)(2,1)S(1)} %get-tuple-element.12), channel_id=1, source_target_pairs={{1,0},{2,1},{3,2},{4,3},{5,4},{6,5},{7,6},{8,7},{9,8},{10,9},{11,1... | collective-permute-start | bytes 2359304 | tf_op jit(solution)/shard_map/ppermute | solution.py:18
  158.2 1.9 collective-permute-start.12
  161.0 3.9 %collective-permute-start.11 = (bf16[256,1536]{1,0:T(8,128)(2,1)}, bf16[256,1536]{1,0:T(8,128)(2,1)S(1)}, u32[]{:S(2)}, u32[]{:S(2)}) collective-permute-start(bf16[256,1536]{1,0:T(8,128)(2,1)} %get-tuple-element.18), channel_id=1, source_target_pairs={{0,2},{1,3},{2,4},{3,5},{4,6},{5,7},{6,8},{7,9},{8,10},{9,11},{10,... | collective-permute-start | bytes 2359304 | tf_op jit(solution)/shard_map/ppermute | solution.py:18
  165.0 1.0 fusion.91
  166.9 27.1 %collective-permute-done.15 = bf16[256,1536]{0,1:T(8,128)(2,1)} collective-permute-done((bf16[256,1536]{0,1:T(8,128)(2,1)S(1)}, bf16[256,1536]{0,1:T(8,128)(2,1)}, u32[]{:S(2)}, u32[]{:S(2)}) %collective-permute-start.15) | collective-permute-done | bytes 786464 | tf_op jit(solution)/shard_map/ppermute | solution.py:18
  194.0 1.9 collective-permute-start.10
  195.9 4.5 %collective-permute-start.9 = (bf16[256,1536]{1,0:T(8,128)(2,1)}, bf16[256,1536]{1,0:T(8,128)(2,1)}, u32[]{:S(2)}, u32[]{:S(2)}) collective-permute-start(bf16[256,1536]{1,0:T(8,128)(2,1)} %get-tuple-element.17), channel_id=1, source_target_pairs={{1,0},{2,1},{3,2},{4,3},{5,4},{6,5},{7,6},{8,7},{9,8},{10,9},{11,1... | collective-permute-start | bytes 2359304 | tf_op jit(solution)/shard_map/ppermute | solution.py:18
  200.5 20.0 %collective-permute-start.8 = (bf16[256,1536]{1,0:T(8,128)(2,1)}, bf16[256,1536]{1,0:T(8,128)(2,1)}, u32[]{:S(2)}, u32[]{:S(2)}) collective-permute-start(bf16[256,1536]{1,0:T(8,128)(2,1)} %get-tuple-element.14), channel_id=1, source_target_pairs={{2,0},{3,1},{4,2},{5,3},{6,4},{7,5},{8,6},{9,7},{10,8},{11,9},{12,... | collective-permute-start | bytes 2359304 | tf_op jit(solution)/shard_map/ppermute | solution.py:18
  221.5 2.3 copy.42
  223.7 7.9 %collective-permute-done.12 = bf16[256,1536]{0,1:T(8,128)(2,1)} collective-permute-done((bf16[256,1536]{0,1:T(8,128)(2,1)S(1)}, bf16[256,1536]{0,1:T(8,128)(2,1)}, u32[]{:S(2)}, u32[]{:S(2)}) %collective-permute-start.12) | collective-permute-done | bytes 786464 | tf_op jit(solution)/shard_map/ppermute | solution.py:18
  231.7 2.3 add_convert_fusion
  234.0 1.2 copy.43
  235.2 17.9 %collective-permute-done.8 = bf16[256,1536]{1,0:T(8,128)(2,1)} collective-permute-done((bf16[256,1536]{1,0:T(8,128)(2,1)}, bf16[256,1536]{1,0:T(8,128)(2,1)}, u32[]{:S(2)}, u32[]{:S(2)}) %collective-permute-start.8) | collective-permute-done | bytes 786464 | tf_op jit(solution)/shard_map/ppermute | solution.py:18
  253.1 3.0 %add_convert_fusion.1 = bf16[256,1536]{1,0:T(8,128)(2,1)} fusion(bf16[256,1536]{1,0:T(8,128)(2,1)S(1)} %collective-permute-done.11, bf16[256,1536]{1,0:T(8,128)(2,1)} %collective-permute-done.10, bf16[256,1536]{1,0:T(8,128)(2,1)S(1)} %get-tuple-element.16, bf16[256,1536]{1,0:T(8,128)(2,1)} %collective-permute-done.9, bf16[256,1536]{1,0:T(8,128)(2,1)} %collective-permute-done.8), kind=kLoop, calls=%fused_computation.98 | loop fusion | flops 3932160 | bytes 4718592 | tf_op jit(solution)/shard_map/convert_element_type | solution.py:151
  (172 shorter events, 46.1 us)
Async XLA Ops:
  0.6 21.1 %copy-start = (bf16[256,1536]{1,0:T(8,128)(2,1)S(1)}, bf16[256,1536]{1,0:T(8,128)(2,1)}, u32[]{:S(2)}) copy-start(bf16[256,1536]{1,0:T(8,128)(2,1)} %param.14) | copy-start | bytes 2359300
  0.6 47.1 %collective-permute-start = (bf16[256,1536]{1,0:T(8,128)(2,1)}, bf16[256,1536]{1,0:T(8,128)(2,1)}, u32[]{:S(2)}, u32[]{:S(2)}) collective-permute-start(bf16[256,1536]{1,0:T(8,128)(2,1)} %param.12), channel_id=1, source_target_pairs={{0,2},{1,3},{2,4},{3,5},{4,6},{5,7},{6,8},{7,9},{8,10},{9,11},{10,... | collective-permute-start | bytes 2359304 | tf_op jit(solution)/shard_map/ppermute | solution.py:18
  4.2 46.6 %collective-permute-start.1 = (bf16[256,1536]{1,0:T(8,128)(2,1)}, bf16[256,1536]{1,0:T(8,128)(2,1)}, u32[]{:S(2)}, u32[]{:S(2)}) collective-permute-start(bf16[256,1536]{1,0:T(8,128)(2,1)} %param.12), channel_id=1, source_target_pairs={{0,1},{1,2},{2,3},{3,4},{4,5},{5,6},{6,7},{7,8},{8,9},{9,10},{10,1... | collective-permute-start | bytes 2359304 | tf_op jit(solution)/shard_map/ppermute | solution.py:18
  6.1 50.5 %collective-permute-start.2 = (bf16[256,1536]{1,0:T(8,128)(2,1)}, bf16[256,1536]{1,0:T(8,128)(2,1)}, u32[]{:S(2)}, u32[]{:S(2)}) collective-permute-start(bf16[256,1536]{1,0:T(8,128)(2,1)} %param.12), channel_id=1, source_target_pairs={{1,0},{2,1},{3,2},{4,3},{5,4},{6,5},{7,6},{8,7},{9,8},{10,9},{11,1... | collective-permute-start | bytes 2359304 | tf_op jit(solution)/shard_map/ppermute | solution.py:18
  10.7 73.6 %collective-permute-start.3 = (bf16[256,1536]{1,0:T(8,128)(2,1)}, bf16[256,1536]{1,0:T(8,128)(2,1)S(1)}, u32[]{:S(2)}, u32[]{:S(2)}) collective-permute-start(bf16[256,1536]{1,0:T(8,128)(2,1)} %param.12), channel_id=1, source_target_pairs={{2,0},{3,1},{4,2},{5,3},{6,4},{7,5},{8,6},{9,7},{10,8},{11,9},{12,... | collective-permute-start | bytes 2359304 | tf_op jit(solution)/shard_map/ppermute | solution.py:18
  13.1 75.6 %collective-permute-start.4 = (bf16[256,1536]{1,0:T(8,128)(2,1)}, bf16[256,1536]{1,0:T(8,128)(2,1)S(1)}, u32[]{:S(2)}, u32[]{:S(2)}) collective-permute-start(bf16[256,1536]{1,0:T(8,128)(2,1)} %param.13), channel_id=1, source_target_pairs={{0,2},{1,3},{2,4},{3,5},{4,6},{5,7},{6,8},{7,9},{8,10},{9,11},{10,... | collective-permute-start | bytes 2359304 | tf_op jit(solution)/shard_map/ppermute | solution.py:18
  21.8 26.0 %copy-start.3 = (bf16[256,1536]{1,0:T(8,128)(2,1)S(1)}, bf16[256,1536]{1,0:T(8,128)(2,1)}, u32[]{:S(2)}) copy-start(bf16[256,1536]{1,0:T(8,128)(2,1)} %param.13) | copy-start | bytes 2359300
  40.6 16.0 %copy-start.2 = (bf16[256,1536]{1,0:T(8,128)(2,1)S(1)}, bf16[256,1536]{1,0:T(8,128)(2,1)}, u32[]{:S(2)}) copy-start(bf16[256,1536]{1,0:T(8,128)(2,1)} %param.12) | copy-start | bytes 2359300
  47.7 41.0 %collective-permute-start.5 = (bf16[256,1536]{1,0:T(8,128)(2,1)S(1)}, bf16[256,1536]{1,0:T(8,128)(2,1)S(1)}, u32[]{:S(2)}, u32[]{:S(2)}) collective-permute-start(bf16[256,1536]{1,0:T(8,128)(2,1)S(1)} %copy-done.3), channel_id=1, source_target_pairs={{0,1},{1,2},{2,3},{3,4},{4,5},{5,6},{6,7},{7,8},{8,9},{9,10},{10,1... | collective-permute-start | bytes 2359304 | tf_op jit(solution)/shard_map/ppermute | solution.py:18
  50.8 38.5 %collective-permute-start.6 = (bf16[256,1536]{1,0:T(8,128)(2,1)S(1)}, bf16[256,1536]{1,0:T(8,128)(2,1)S(1)}, u32[]{:S(2)}, u32[]{:S(2)}) collective-permute-start(bf16[256,1536]{1,0:T(8,128)(2,1)S(1)} %copy-done.3), channel_id=1, source_target_pairs={{1,0},{2,1},{3,2},{4,3},{5,4},{6,5},{7,6},{8,7},{9,8},{10,9},{11,1... | collective-permute-start | bytes 2359304 | tf_op jit(solution)/shard_map/ppermute | solution.py:18
  56.7 27.6 %copy-start.1 = (bf16[256,1536]{1,0:T(8,128)(2,1)S(1)}, bf16[256,1536]{1,0:T(8,128)(2,1)}, u32[]{:S(2)}) copy-start(bf16[256,1536]{1,0:T(8,128)(2,1)} %param.11) | copy-start | bytes 2359300
  56.7 50.6 %collective-permute-start.7 = (bf16[256,1536]{1,0:T(8,128)(2,1)S(1)}, bf16[256,1536]{1,0:T(8,128)(2,1)S(1)}, u32[]{:S(2)}, u32[]{:S(2)}) collective-permute-start(bf16[256,1536]{1,0:T(8,128)(2,1)S(1)} %copy-done.3), channel_id=1, source_target_pairs={{2,0},{3,1},{4,2},{5,3},{6,4},{7,5},{8,6},{9,7},{10,8},{11,9},{12,... | collective-permute-start | bytes 2359304 | tf_op jit(solution)/shard_map/ppermute | solution.py:18
  89.8 17.6 %copy-start.15 = (bf16[256,128]{0,1:T(8,128)(2,1)S(1)}, bf16[256,128]{0,1:T(8,128)(2,1)}, u32[]{:S(2)}) copy-start(bf16[256,128]{0,1:T(8,128)(2,1)} %copy.44) | copy-start | bytes 196612
  109.6 0.8 copy-start.14
  112.7 0.8 copy-start.13
  115.7 0.8 copy-start.12
  118.8 0.8 copy-start.11
  122.1 0.8 copy-start.10
  125.2 0.8 copy-start.9
  128.2 0.8 copy-start.8
  130.0 0.8 copy-start.7
  131.8 0.8 copy-start.6
  133.6 0.8 copy-start.5
  135.4 0.8 copy-start.4
  146.4 47.6 %collective-permute-start.15 = (bf16[256,1536]{0,1:T(8,128)(2,1)S(1)}, bf16[256,1536]{0,1:T(8,128)(2,1)}, u32[]{:S(2)}, u32[]{:S(2)}) collective-permute-start(bf16[256,1536]{0,1:T(8,128)(2,1)S(1)} %get-tuple-element.13), channel_id=1, source_target_pairs={{0,2},{1,3},{2,4},{3,5},{4,6},{5,7},{6,8},{7,9},{8,10},{9,11},{10,... | collective-permute-start | bytes 2359304 | tf_op jit(solution)/shard_map/ppermute | solution.py:18
  150.7 45.2 %collective-permute-start.14 = (bf16[256,1536]{0,1:T(8,128)(2,1)S(1)}, bf16[256,1536]{0,1:T(8,128)(2,1)}, u32[]{:S(2)}, u32[]{:S(2)}) collective-permute-start(bf16[256,1536]{0,1:T(8,128)(2,1)S(1)} %get-tuple-element.10), channel_id=1, source_target_pairs={{0,1},{1,2},{2,3},{3,4},{4,5},{5,6},{6,7},{7,8},{8,9},{9,10},{10,1... | collective-permute-start | bytes 2359304 | tf_op jit(solution)/shard_map/ppermute | solution.py:18
  152.7 47.8 %collective-permute-start.13 = (bf16[256,1536]{0,1:T(8,128)(2,1)S(1)}, bf16[256,1536]{0,1:T(8,128)(2,1)}, u32[]{:S(2)}, u32[]{:S(2)}) collective-permute-start(bf16[256,1536]{0,1:T(8,128)(2,1)S(1)} %get-tuple-element.12), channel_id=1, source_target_pairs={{1,0},{2,1},{3,2},{4,3},{5,4},{6,5},{7,6},{8,7},{9,8},{10,9},{11,1... | collective-permute-start | bytes 2359304 | tf_op jit(solution)/shard_map/ppermute | solution.py:18
  158.2 73.5 %collective-permute-start.12 = (bf16[256,1536]{0,1:T(8,128)(2,1)S(1)}, bf16[256,1536]{0,1:T(8,128)(2,1)}, u32[]{:S(2)}, u32[]{:S(2)}) collective-permute-start(bf16[256,1536]{0,1:T(8,128)(2,1)S(1)} %get-tuple-element.9), channel_id=1, source_target_pairs={{2,0},{3,1},{4,2},{5,3},{6,4},{7,5},{8,6},{9,7},{10,8},{11,9},{12,... | collective-permute-start | bytes 2359304 | tf_op jit(solution)/shard_map/ppermute | solution.py:18
  161.0 74.1 %collective-permute-start.11 = (bf16[256,1536]{1,0:T(8,128)(2,1)}, bf16[256,1536]{1,0:T(8,128)(2,1)S(1)}, u32[]{:S(2)}, u32[]{:S(2)}) collective-permute-start(bf16[256,1536]{1,0:T(8,128)(2,1)} %get-tuple-element.18), channel_id=1, source_target_pairs={{0,2},{1,3},{2,4},{3,5},{4,6},{5,7},{6,8},{7,9},{8,10},{9,11},{10,... | collective-permute-start | bytes 2359304 | tf_op jit(solution)/shard_map/ppermute | solution.py:18
  194.0 41.2 %collective-permute-start.10 = (bf16[256,1536]{1,0:T(8,128)(2,1)}, bf16[256,1536]{1,0:T(8,128)(2,1)}, u32[]{:S(2)}, u32[]{:S(2)}) collective-permute-start(bf16[256,1536]{1,0:T(8,128)(2,1)} %get-tuple-element.15), channel_id=1, source_target_pairs={{0,1},{1,2},{2,3},{3,4},{4,5},{5,6},{6,7},{7,8},{8,9},{9,10},{10,1... | collective-permute-start | bytes 2359304 | tf_op jit(solution)/shard_map/ppermute | solution.py:18
  195.9 39.2 %collective-permute-start.9 = (bf16[256,1536]{1,0:T(8,128)(2,1)}, bf16[256,1536]{1,0:T(8,128)(2,1)}, u32[]{:S(2)}, u32[]{:S(2)}) collective-permute-start(bf16[256,1536]{1,0:T(8,128)(2,1)} %get-tuple-element.17), channel_id=1, source_target_pairs={{1,0},{2,1},{3,2},{4,3},{5,4},{6,5},{7,6},{8,7},{9,8},{10,9},{11,1... | collective-permute-start | bytes 2359304 | tf_op jit(solution)/shard_map/ppermute | solution.py:18
  200.5 52.6 %collective-permute-start.8 = (bf16[256,1536]{1,0:T(8,128)(2,1)}, bf16[256,1536]{1,0:T(8,128)(2,1)}, u32[]{:S(2)}, u32[]{:S(2)}) collective-permute-start(bf16[256,1536]{1,0:T(8,128)(2,1)} %get-tuple-element.14), channel_id=1, source_target_pairs={{2,0},{3,1},{4,2},{5,3},{6,4},{7,5},{8,6},{9,7},{10,8},{11,9},{12,... | collective-permute-start | bytes 2359304 | tf_op jit(solution)/shard_map/ppermute | solution.py:18
where the time goes:
time: 258 us; the launch traced here: 256 us
  starting transfers between devices  87.2 us (34%)
  waiting for transfers between devices  82.1 us (32%)
  local copies, waits for them, and re-layouts  40 us (16%)
  matrix products  33.1 us (13%)
  other arithmetic  12.2 us (5%)
    ppermute x16, starting transfers between devices, from_behind(): lax.ppermute(value, axis, [(source, source + steps) for source in range(f...  87.2 us
    ppermute x16, waiting for transfers between devices, from_behind(): lax.ppermute(value, axis, [(source, source + steps) for source in range(f...  82.1 us
    unnamed x66, local copies, waits for them, and re-layouts  34 us
    dot_general x12, matrix products, group_grads(): jnp.einsum('qk,kd->qd', grad_scores, key_head, preferred_element_type=jnp...  11.4 us
  transfers between devices with their start and end apart: 16, of which 6 were waited for; matrix products, arithmetic and copies ran while one was open for 17% of the time, Pallas kernels for 0%

commit v1 on v0

v1 whole, which is shorter than its diff:
```python
import functools
import math

import jax
import jax.numpy as jnp
from jax import lax
from jax.experimental import pallas as pl
from jax.experimental.pallas import tpu as pltpu
from jax.sharding import PartitionSpec as P

HDIM = 128
BLOCK = 64
REACH = 2
FRAMES = 2
BANDS = 2
SLOTS = 2 * REACH + 1
BLOCKS = FRAMES * BANDS
TOK = BLOCKS * BLOCK
MESH = pl.DeviceIdType.MESH
AHEAD = 12

OWN, SIB, PARTNER, EXTRA, RELAY = range(5)


def place(tm_count):
    here = lax.axis_index("tm")
    core = lax.rem(here, 2)
    half = lax.rem(here // 2, 2)
    column = here // 4
    columns = tm_count // 4
    down, up = column > 0, column < columns - 1
    even = half == 0
    has_relay = (even & down) | (~even & up)
    has_target = (even & up) | (~even & down)
    return here, core, half, down, up, has_relay, has_target


def slot_bias(block_list, tm_count):
    here, core, half, _, _, _, _ = place(tm_count)
    shape = (SLOTS * BLOCKS, BLOCKS, FRAMES * SLOTS * 3)
    key_block = lax.broadcasted_iota(jnp.int32, shape, 0)
    query_block = lax.broadcasted_iota(jnp.int32, shape, 1)
    slot = key_block // BLOCKS
    offset = jnp.where(
        slot == OWN, REACH,
        jnp.where(
            slot == SIB, 3 - 2 * core,
            jnp.where(
                slot == PARTNER, 4 - 4 * half,
                jnp.where(slot == EXTRA, 1 + 2 * core, 4 * half),
            ),
        ),
    )
    frame = key_block // BANDS % FRAMES
    band = key_block % BANDS
    cand = (offset * FRAMES + frame) * 3 + band - query_block % BANDS + 1
    group = here + offset - REACH
    exists = (group >= 0) & (group < tm_count)
    hit = exists & (lax.broadcasted_iota(jnp.int32, shape, 2) == cand)
    mine = (slot == OWN) & (key_block % BLOCKS == query_block)
    hits = (hit & (block_list > 0)[None]) | mine
    listed = jnp.max(hits.astype(jnp.float32), axis=2, keepdims=True)
    listed = jnp.broadcast_to(listed, (SLOTS * BLOCKS, BLOCKS, BLOCK))
    return jnp.where(listed > 0.5, 0.0, -jnp.inf).reshape(SLOTS * BLOCKS, TOK)


def kernel(
    tm_count, heads,
    q_ref, k_ref, v_ref, do_ref, bias_ref,
    dq_ref, dk_ref, dv_ref,
    kv, back_out, back_in, own_acc, partner_acc, relay_acc,
    fwd_send, fwd_recv, back_send, back_recv,
):
    here, core, half, down, up, has_relay, has_target = place(tm_count)
    sibling = here + 1 - 2 * core
    partner = here + 2 - 4 * half
    target = here + 4 - 8 * half
    source = here - 4 + 8 * half
    same = half == core
    scale = HDIM ** -0.5
    scale2 = scale * math.log2(math.e)

    barrier = pltpu.get_barrier_semaphore()

    def greet(device):
        pl.semaphore_signal(barrier, inc=1, device_id={"tm": device}, device_id_type=MESH)

    greet(sibling)
    greet(partner)

    @pl.when(down)
    def _():
        greet(here - 4)

    @pl.when(up)
    def _():
        greet(here + 4)

    def columns(h):
        return pl.ds(pl.multiple_of(h * HDIM, HDIM), HDIM)

    def pack(h, carry):
        kv[OWN, h, 0:TOK, :] = k_ref[:, columns(h)]
        kv[OWN, h, TOK:2 * TOK, :] = v_ref[:, columns(h)]
        return carry

    lax.fori_loop(0, heads, pack, 0)

    @pl.when(~has_relay)
    def _():
        def clear(h, carry):
            kv[RELAY, h] = jnp.zeros((2 * TOK, HDIM), jnp.bfloat16)
            return carry

        lax.fori_loop(0, heads, clear, 0)

    @pl.when(same & ~has_relay)
    def _():
        def clear(h, carry):
            kv[EXTRA, h] = jnp.zeros((2 * TOK, HDIM), jnp.bfloat16)
            return carry

        lax.fori_loop(0, heads, clear, 0)

    pl.semaphore_wait(barrier, 2 + down.astype(jnp.int32) + up.astype(jnp.int32))

    def forward(slot_from, slot_to, h, device):
        return pltpu.make_async_remote_copy(
            src_ref=kv.at[slot_from, h],
            dst_ref=kv.at[slot_to, h],
            send_sem=fwd_send.at[slot_to - 1, h],
            recv_sem=fwd_recv.at[slot_to - 1, h],
            device_id={"tm": device},
            device_id_type=MESH,
        )

    def backward(slot, h, device):
        return pltpu.make_async_remote_copy(
            src_ref=back_out.at[slot - 1, h],
            dst_ref=back_in.at[slot - 1, h],
            send_sem=back_send.at[slot - 1, h],
            recv_sem=back_recv.at[slot - 1, h],
            device_id={"tm": device},
            device_id_type=MESH,
        )

    def send_own(h):
        forward(OWN, PARTNER, h, partner).start()
        forward(OWN, SIB, h, sibling).start()

    def first(h, carry):
        send_own(h)
        return carry

    lax.fori_loop(0, min(AHEAD, heads), first, 0)

    def pass_partner(h):
        forward(OWN, PARTNER, h, partner).wait_recv()

        @pl.when(has_target)
        def _():
            forward(PARTNER, RELAY, h, target).start()

        @pl.when(same)
        def _():
            forward(PARTNER, EXTRA, h, sibling).start()

    def pass_relay(h):
        @pl.when(has_relay)
        def _():
            forward(PARTNER, RELAY, h, target).wait_recv()

        @pl.when(has_relay & ~same)
        def _():
            forward(RELAY, EXTRA, h, sibling).start()

    def compute(h):
        forward(OWN, SIB, h, sibling).wait_recv()

        @pl.when(has_relay | ~same)
        def _():
            forward(PARTNER, EXTRA, h, sibling).wait_recv()

        query = q_ref[:, columns(h)]
        grad = do_ref[:, columns(h)]
        scores, probs = [], []
        top = None
        for slot in range(SLOTS):
            raw = lax.dot_general(
                kv[slot, h, 0:TOK, :], query, (((1,), (1,)), ((), ())),
                preferred_element_type=jnp.float32,
            )
            parts = [
                raw[b * BLOCK:(b + 1) * BLOCK] * scale2
                + bias_ref[slot * BLOCKS + b:slot * BLOCKS + b + 1, :]
                for b in range(BLOCKS)
            ]
            score = jnp.concatenate(parts, axis=0)
            scores.append(score)
            peak = jnp.max(score, axis=0, keepdims=True)
            top = peak if top is None else jnp.maximum(top, peak)
        total = jnp.zeros((1, TOK), jnp.float32)
        dot = jnp.zeros((1, TOK), jnp.float32)
        weights = []
        for slot in range(SLOTS):
            prob = lax.dot_general(
                kv[slot, h, TOK:2 * TOK, :], grad, (((1,), (1,)), ((), ())),
                preferred_element_type=jnp.float32,
            )
            weight = jnp.exp2(scores[slot] - top)
            total = total + jnp.sum(weight, axis=0, keepdims=True)
            dot = dot + jnp.sum(weight * prob, axis=0, keepdims=True)
            weights.append(weight)
            probs.append(prob)
        inverse = 1.0 / total
        delta = dot * inverse
        query_grad = jnp.zeros((TOK, HDIM), jnp.float32)
        for slot in range(SLOTS):
            weight = weights[slot] * inverse
            low = weight.astype(jnp.bfloat16)
            grad_score = (weight * (probs[slot] - delta)).astype(jnp.bfloat16)
            value_part = jnp.dot(low, grad, preferred_element_type=jnp.float32)
            key_part = jnp.dot(grad_score, query, preferred_element_type=jnp.float32) * scale
            query_grad = query_grad + lax.dot_general(
                grad_score, kv[slot, h, 0:TOK, :], (((0,), (0,)), ((), ())),
                preferred_element_type=jnp.float32,
            )
            if slot in (SIB, EXTRA):
                back_out[slot - 1, h, 0:TOK, :] = key_part.astype(jnp.bfloat16)
                back_out[slot - 1, h, TOK:2 * TOK, :] = value_part.astype(jnp.bfloat16)
            else:
                acc = {OWN: own_acc, PARTNER: partner_acc, RELAY: relay_acc}[slot]
                acc[h, 0:TOK, :] = key_part
                acc[h, TOK:2 * TOK, :] = value_part
        dq_ref[:, columns(h)] = (query_grad * scale).astype(jnp.bfloat16)

        backward(SIB, h, sibling).start()

        @pl.when(has_relay | ~same)
        def _():
            backward(EXTRA, h, sibling).start()

    def return_relay(h):
        @pl.when(same)
        def _():
            backward(EXTRA, h, sibling).wait_recv()
            partner_acc[h] = partner_acc[h] + back_in[EXTRA - 1, h].astype(jnp.float32)

        @pl.when(has_relay & ~same)
        def _():
            backward(EXTRA, h, sibling).wait_recv()
            relay_acc[h] = relay_acc[h] + back_in[EXTRA - 1, h].astype(jnp.float32)

        @pl.when(has_relay)
        def _():
            back_out[RELAY - 1, h] = relay_acc[h].astype(jnp.bfloat16)
            backward(RELAY, h, source).start()

    def return_partner(h):
        @pl.when(has_target)
        def _():
            backward(RELAY, h, source).wait_recv()
            partner_acc[h] = partner_acc[h] + back_in[RELAY - 1, h].astype(jnp.float32)

        back_out[PARTNER - 1, h] = partner_acc[h].astype(jnp.bfloat16)
        backward(PARTNER, h, partner).start()

    def finish(h):
        backward(SIB, h, sibling).wait_recv()
        backward(PARTNER, h, partner).wait_recv()
        done = (
            own_acc[h]
            + back_in[SIB - 1, h].astype(jnp.float32)
            + back_in[PARTNER - 1, h].astype(jnp.float32)
        ).astype(jnp.bfloat16)
        dk_ref[:, columns(h)] = done[0:TOK]
        dv_ref[:, columns(h)] = done[TOK:2 * TOK]

    stages = (pass_partner, pass_relay, compute, return_relay, return_partner, finish)

    def step(at, carry):
        if AHEAD < heads:
            @pl.when(at + AHEAD < heads)
            def _():
                send_own(at + AHEAD)

        for lag, stage in enumerate(stages):
            @pl.when((at >= lag) & (at < heads + lag))
            def _(stage=stage, lag=lag):
                stage(at - lag)

        return carry

    lax.fori_loop(0, heads + len(stages) - 1, step, 0)

    def drain(h, carry):
        forward(OWN, PARTNER, h, partner).wait_send()
        forward(OWN, SIB, h, sibling).wait_send()
        backward(SIB, h, sibling).wait_send()
        backward(PARTNER, h, partner).wait_send()

        @pl.when(has_target)
        def _():
            forward(PARTNER, RELAY, h, target).wait_send()

        @pl.when(has_relay)
        def _():
            backward(RELAY, h, source).wait_send()

        @pl.when(same | has_relay)
        def _():
            forward(PARTNER, EXTRA, h, sibling).wait_send()

        @pl.when(~same | has_relay)
        def _():
            backward(EXTRA, h, sibling).wait_send()

        return carry

    lax.fori_loop(0, heads, drain, 0)


def local(tm_count, queries, keys, values, grad_out, block_list):
    heads = queries.shape[1] // HDIM
    bias = slot_bias(block_list, tm_count)
    out = jax.ShapeDtypeStruct(queries.shape, jnp.bfloat16)
    vmem = pl.BlockSpec(memory_space=pltpu.VMEM)
    pair = (heads, 2 * TOK, HDIM)
    return pl.pallas_call(
        functools.partial(kernel, tm_count, heads),
        out_shape=(out, out, out),
        in_specs=[vmem] * 5,
        out_specs=(vmem, vmem, vmem),
        scratch_shapes=[
            pltpu.VMEM((SLOTS,) + pair, jnp.bfloat16),
            pltpu.VMEM((SLOTS - 1,) + pair, jnp.bfloat16),
            pltpu.VMEM((SLOTS - 1,) + pair, jnp.bfloat16),
            pltpu.VMEM(pair, jnp.float32),
            pltpu.VMEM(pair, jnp.float32),
            pltpu.VMEM(pair, jnp.float32),
            pltpu.SemaphoreType.DMA((SLOTS - 1, heads)),
            pltpu.SemaphoreType.DMA((SLOTS - 1, heads)),
            pltpu.SemaphoreType.DMA((SLOTS - 1, heads)),
            pltpu.SemaphoreType.DMA((SLOTS - 1, heads)),
        ],
        compiler_params=pltpu.CompilerParams(
            collective_id=0, has_side_effects=True, vmem_limit_bytes=56 * 2**20
        ),
    )(queries, keys, values, grad_out, bias)


def solution(mesh):
    placed = P(("group", "tm"), None)
    return jax.shard_map(
        functools.partial(local, mesh.shape["tm"]),
        mesh=mesh,
        in_specs=(placed,) * 5,
        out_specs=(placed,) * 3,
        check_vma=False,
    )
```

time: 258 us -> 95.1 us (0.37)
  the two profiles are of different devices: /device:TPU:16 before, /device:TPU:0 now
where the time goes in v1:
time: 95.1 us; the launch traced here: 94.8 us
  Pallas kernels  87.8 us (92%)
  local copies, waits for them, and re-layouts  5.89 us (6%)
    pallas_call x1, Pallas kernels, local(): pl.pallas_call(functools.partial(kernel, tm_count, heads), out_shape=(out...  87.8 us
    unnamed x9, local copies, waits for them, and re-layouts  5.11 us

profile of v1, /device:TPU:0, one launch (start us, length us, event | category | flops | bytes accessed | tf_op | source)
XLA Modules:
  0.0 94.8 jit_solution(2164236140022168276)
XLA Ops:
  0.7 0.0 copy-start.2
  0.7 0.7 copy-done.2
  1.4 0.4 convert_reduce_fusion
  1.8 0.1 broadcast_in_dim.41
  1.9 0.7 select_n.75.bias_ref
  2.6 87.8 %shard_map.76 = (bf16[256,1536]{1,0:T(8,128)(2,1)}, bf16[256,1536]{1,0:T(8,128)(2,1)}, bf16[256,1536]{1,0:T(8,128)(2,1)}) custom-call(bf16[256,1536]{1,0:T(8,128)(2,1)} %q_ref.1, bf16[256,1536]{1,0:T(8,128)(2,1)} %k_ref.1, bf16[256,1536]{1,0:T(8,128)(2,1)} %v_ref.1, bf16[256,1536]{1,0:T(8,128)(2,1)} %do_ref.1, f32[20,256]{1,0:T(8,128)} %select_n.75.bias_ref), custom_call_target="tpu_custom_call" | custom-call | tf_op jit(solution)/shard_map/pallas_call | solution.py:329
  90.4 0.0 copy-start.1
  90.4 2.1 %copy.11 = bf16[256,1536]{1,0:T(8,128)(2,1)} copy(bf16[256,1536]{1,0:T(8,128)(2,1)} %get-tuple-element.20) | data formatting | bytes 1572864
  92.5 0.0 copy-done.1
  92.5 0.0 copy-start
  92.5 0.9 copy.12
  93.4 0.5 copy-done
  94.0 0.9 copy.13
  (10 shorter events, 0.0 us)
Async XLA Ops:
  0.7 0.7 copy-start.2
  90.4 2.1 %copy-start.1 = (bf16[256,1536]{1,0:T(8,128)(2,1)S(1)}, bf16[256,1536]{1,0:T(8,128)(2,1)}, u32[]{:S(2)}) copy-start(bf16[256,1536]{1,0:T(8,128)(2,1)} %get-tuple-element.21) | copy-start | bytes 2359300
  92.5 1.4 %copy-start = (bf16[256,1536]{1,0:T(8,128)(2,1)S(1)}, bf16[256,1536]{1,0:T(8,128)(2,1)}, u32[]{:S(2)}) copy-start(bf16[256,1536]{1,0:T(8,128)(2,1)} %get-tuple-element.22) | copy-start | bytes 2359300

commit v2 on v1

--- a/solution.py
+++ b/solution.py
@@ -276,7 +276,9 @@
         dk_ref[:, columns(h)] = done[0:TOK]
         dv_ref[:, columns(h)] = done[TOK:2 * TOK]
 
-    stages = (pass_partner, pass_relay, compute, return_relay, return_partner, finish)
+    stages = (
+        (0, pass_partner), (1, pass_relay), (6, return_partner), (4, return_relay), (2, compute),
+    )
 
     def step(at, carry):
         if AHEAD < heads:
@@ -284,14 +286,20 @@
             def _():
                 send_own(at + AHEAD)
 
-        for lag, stage in enumerate(stages):
+        for lag, stage in stages:
             @pl.when((at >= lag) & (at < heads + lag))
             def _(stage=stage, lag=lag):
                 stage(at - lag)
 
         return carry
 
-    lax.fori_loop(0, heads + len(stages) - 1, step, 0)
+    lax.fori_loop(0, heads + max(lag for lag, _ in stages), step, 0)
+
+    def last(h, carry):
+        finish(h)
+        return carry
+
+    lax.fori_loop(0, heads, last, 0)
 
     def drain(h, carry):
         forward(OWN, PARTNER, h, partner).wait_send()

time: 95.1 us -> 84.8 us (0.89)
  Pallas kernels: 87.8 us -> 77.5 us
    pallas_call x1, Pallas kernels: 87.8 us -> 77.5 us  [local(): pl.pallas_call(functools.partial(kernel, tm_count, heads), out_shape=(out...]
where the time goes in v2:
time: 84.8 us; the launch traced here: 84.6 us
  Pallas kernels  77.5 us (91%)
  local copies, waits for them, and re-layouts  5.89 us (7%)
    pallas_call x1, Pallas kernels, local(): pl.pallas_call(functools.partial(kernel, tm_count, heads), out_shape=(out...  77.5 us
    unnamed x9, local copies, waits for them, and re-layouts  5.11 us

profile of v2, /device:TPU:0, one launch (start us, length us, event | category | flops | bytes accessed | tf_op | source)
XLA Modules:
  0.0 84.6 jit_solution(9051226469862063412)
XLA Ops:
  0.7 0.0 copy-start.2
  0.7 0.7 copy-done.2
  1.4 0.4 convert_reduce_fusion
  1.8 0.1 broadcast_in_dim.41
  1.9 0.7 select_n.75.bias_ref
  2.6 77.5 %shard_map.76 = (bf16[256,1536]{1,0:T(8,128)(2,1)}, bf16[256,1536]{1,0:T(8,128)(2,1)}, bf16[256,1536]{1,0:T(8,128)(2,1)}) custom-call(bf16[256,1536]{1,0:T(8,128)(2,1)} %q_ref.1, bf16[256,1536]{1,0:T(8,128)(2,1)} %k_ref.1, bf16[256,1536]{1,0:T(8,128)(2,1)} %v_ref.1, bf16[256,1536]{1,0:T(8,128)(2,1)} %do_ref.1, f32[20,256]{1,0:T(8,128)} %select_n.75.bias_ref), custom_call_target="tpu_custom_call" | custom-call | tf_op jit(solution)/shard_map/pallas_call | solution.py:337
  80.2 0.0 copy-start.1
  80.2 2.1 %copy.11 = bf16[256,1536]{1,0:T(8,128)(2,1)} copy(bf16[256,1536]{1,0:T(8,128)(2,1)} %get-tuple-element.20) | data formatting | bytes 1572864
  82.3 0.0 copy-done.1
  82.3 0.0 copy-start
  82.3 0.9 %copy.12 = bf16[256,1536]{1,0:T(8,128)(2,1)} copy(bf16[256,1536]{1,0:T(8,128)(2,1)S(1)} %copy-done.1) | data formatting | bytes 1572864
  83.2 0.5 copy-done
  83.7 0.9 %copy.13 = bf16[256,1536]{1,0:T(8,128)(2,1)} copy(bf16[256,1536]{1,0:T(8,128)(2,1)S(1)} %copy-done) | data formatting | bytes 1572864
  (10 shorter events, 0.0 us)
Async XLA Ops:
  0.7 0.7 copy-start.2
  80.2 2.1 %copy-start.1 = (bf16[256,1536]{1,0:T(8,128)(2,1)S(1)}, bf16[256,1536]{1,0:T(8,128)(2,1)}, u32[]{:S(2)}) copy-start(bf16[256,1536]{1,0:T(8,128)(2,1)} %get-tuple-element.21) | copy-start | bytes 2359300
  82.3 1.4 %copy-start = (bf16[256,1536]{1,0:T(8,128)(2,1)S(1)}, bf16[256,1536]{1,0:T(8,128)(2,1)}, u32[]{:S(2)}) copy-start(bf16[256,1536]{1,0:T(8,128)(2,1)} %get-tuple-element.22) | copy-start | bytes 2359300

commit v3 on v2

--- a/solution.py
+++ b/solution.py
@@ -17,7 +17,7 @@
 BLOCKS = FRAMES * BANDS
 TOK = BLOCKS * BLOCK
 MESH = pl.DeviceIdType.MESH
-AHEAD = 12
+AHEAD = 4
 
 OWN, SIB, PARTNER, EXTRA, RELAY = range(5)
 
@@ -68,8 +68,8 @@
     tm_count, heads,
     q_ref, k_ref, v_ref, do_ref, bias_ref,
     dq_ref, dk_ref, dv_ref,
-    kv, back_out, back_in, own_acc, partner_acc, relay_acc,
-    fwd_send, fwd_recv, back_send, back_recv,
+    q_buf, do_buf, kv, back_out, back_in, own_acc, partner_acc, relay_acc,
+    row_sem, load_sem, fwd_send, fwd_recv, back_send, back_recv,
 ):
     here, core, half, down, up, has_relay, has_target = place(tm_count)
     sibling = here + 1 - 2 * core
@@ -99,12 +99,25 @@
     def columns(h):
         return pl.ds(pl.multiple_of(h * HDIM, HDIM), HDIM)
 
-    def pack(h, carry):
-        kv[OWN, h, 0:TOK, :] = k_ref[:, columns(h)]
-        kv[OWN, h, TOK:2 * TOK, :] = v_ref[:, columns(h)]
-        return carry
-
-    lax.fori_loop(0, heads, pack, 0)
+    def load(which, ref, h):
+        return pltpu.make_async_copy(
+            ref.at[:, columns(h)],
+            kv.at[OWN, h, pl.ds(which * TOK, TOK)],
+            load_sem.at[which, h],
+        )
+
+    def begin(h, carry):
+        load(0, k_ref, h).start()
+        load(1, v_ref, h).start()
+        return carry
+
+    lax.fori_loop(0, heads, begin, 0)
+    rows = (
+        pltpu.make_async_copy(q_ref, q_buf, row_sem.at[0]),
+        pltpu.make_async_copy(do_ref, do_buf, row_sem.at[1]),
+    )
+    for row in rows:
+        row.start()
 
     @pl.when(~has_relay)
     def _():
@@ -145,6 +158,8 @@
         )
 
     def send_own(h):
+        load(0, k_ref, h).wait()
+        load(1, v_ref, h).wait()
         forward(OWN, PARTNER, h, partner).start()
         forward(OWN, SIB, h, sibling).start()
 
@@ -154,6 +169,9 @@
 
     lax.fori_loop(0, min(AHEAD, heads), first, 0)
 
+    for row in rows:
+        row.wait()
+
     def pass_partner(h):
         forward(OWN, PARTNER, h, partner).wait_recv()
 
@@ -181,8 +199,8 @@
         def _():
             forward(PARTNER, EXTRA, h, sibling).wait_recv()
 
-        query = q_ref[:, columns(h)]
-        grad = do_ref[:, columns(h)]
+        query = q_buf[:, columns(h)]
+        grad = do_buf[:, columns(h)]
         scores, probs = [], []
         top = None
         for slot in range(SLOTS):
@@ -337,15 +355,19 @@
     return pl.pallas_call(
         functools.partial(kernel, tm_count, heads),
         out_shape=(out, out, out),
-        in_specs=[vmem] * 5,
+        in_specs=[pl.BlockSpec(memory_space=pl.ANY)] * 4 + [vmem],
         out_specs=(vmem, vmem, vmem),
         scratch_shapes=[
+            pltpu.VMEM(queries.shape, jnp.bfloat16),
+            pltpu.VMEM(queries.shape, jnp.bfloat16),
             pltpu.VMEM((SLOTS,) + pair, jnp.bfloat16),
             pltpu.VMEM((SLOTS - 1,) + pair, jnp.bfloat16),
             pltpu.VMEM((SLOTS - 1,) + pair, jnp.bfloat16),
             pltpu.VMEM(pair, jnp.float32),
             pltpu.VMEM(pair, jnp.float32),
             pltpu.VMEM(pair, jnp.float32),
+            pltpu.SemaphoreType.DMA((2,)),
+            pltpu.SemaphoreType.DMA((2, heads)),
             pltpu.SemaphoreType.DMA((SLOTS - 1, heads)),
             pltpu.SemaphoreType.DMA((SLOTS - 1, heads)),
             pltpu.SemaphoreType.DMA((SLOTS - 1, heads)),

time: 84.8 us -> 84 us (level)
    pallas_call x1, Pallas kernels: 77.5 us -> 76.7 us  [local(): pl.pallas_call(functools.partial(kernel, tm_count, heads), out_shape=(out...]
where the time goes in v3:
time: 84 us; the launch traced here: 83.7 us
  Pallas kernels  76.7 us (91%)
  local copies, waits for them, and re-layouts  5.89 us (7%)
    pallas_call x1, Pallas kernels, local(): pl.pallas_call(functools.partial(kernel, tm_count, heads), out_shape=(out...  76.7 us
    unnamed x9, local copies, waits for them, and re-layouts  5.11 us

profile of v3, /device:TPU:0, one launch (start us, length us, event | category | flops | bytes accessed | tf_op | source)
XLA Modules:
  0.0 83.7 jit_solution(10151953772412644347)
XLA Ops:
  0.7 0.0 copy-start.2
  0.7 0.7 copy-done.2
  1.4 0.4 convert_reduce_fusion
  1.8 0.1 broadcast_in_dim.41
  1.9 0.7 select_n.75.bias_ref
  2.6 76.7 %shard_map.76 = (bf16[256,1536]{1,0:T(8,128)(2,1)}, bf16[256,1536]{1,0:T(8,128)(2,1)}, bf16[256,1536]{1,0:T(8,128)(2,1)}) custom-call(bf16[256,1536]{1,0:T(8,128)(2,1)} %q_ref.1, bf16[256,1536]{1,0:T(8,128)(2,1)} %k_ref.1, bf16[256,1536]{1,0:T(8,128)(2,1)} %v_ref.1, bf16[256,1536]{1,0:T(8,128)(2,1)} %do_ref.1, f32[20,256]{1,0:T(8,128)} %select_n.75.bias_ref), custom_call_target="tpu_custom_call" | custom-call | tf_op jit(solution)/shard_map/pallas_call | solution.py:355
  79.3 0.0 copy-start.1
  79.3 2.1 %copy.11 = bf16[256,1536]{1,0:T(8,128)(2,1)} copy(bf16[256,1536]{1,0:T(8,128)(2,1)} %get-tuple-element.20) | data formatting | bytes 1572864
  81.4 0.0 copy-done.1
  81.4 0.0 copy-start
  81.4 0.9 %copy.12 = bf16[256,1536]{1,0:T(8,128)(2,1)} copy(bf16[256,1536]{1,0:T(8,128)(2,1)S(1)} %copy-done.1) | data formatting | bytes 1572864
  82.3 0.5 copy-done
  82.9 0.9 %copy.13 = bf16[256,1536]{1,0:T(8,128)(2,1)} copy(bf16[256,1536]{1,0:T(8,128)(2,1)S(1)} %copy-done) | data formatting | bytes 1572864
  (10 shorter events, 0.0 us)
Async XLA Ops:
  0.7 0.7 copy-start.2
  79.3 2.1 %copy-start.1 = (bf16[256,1536]{1,0:T(8,128)(2,1)S(1)}, bf16[256,1536]{1,0:T(8,128)(2,1)}, u32[]{:S(2)}) copy-start(bf16[256,1536]{1,0:T(8,128)(2,1)} %get-tuple-element.21) | copy-start | bytes 2359300
  81.4 1.4 %copy-start = (bf16[256,1536]{1,0:T(8,128)(2,1)S(1)}, bf16[256,1536]{1,0:T(8,128)(2,1)}, u32[]{:S(2)}) copy-start(bf16[256,1536]{1,0:T(8,128)(2,1)} %get-tuple-element.22) | copy-start | bytes 2359300

commit v4 on v3

--- a/solution.py
+++ b/solution.py
@@ -35,41 +35,12 @@
     return here, core, half, down, up, has_relay, has_target
 
 
-def slot_bias(block_list, tm_count):
-    here, core, half, _, _, _, _ = place(tm_count)
-    shape = (SLOTS * BLOCKS, BLOCKS, FRAMES * SLOTS * 3)
-    key_block = lax.broadcasted_iota(jnp.int32, shape, 0)
-    query_block = lax.broadcasted_iota(jnp.int32, shape, 1)
-    slot = key_block // BLOCKS
-    offset = jnp.where(
-        slot == OWN, REACH,
-        jnp.where(
-            slot == SIB, 3 - 2 * core,
-            jnp.where(
-                slot == PARTNER, 4 - 4 * half,
-                jnp.where(slot == EXTRA, 1 + 2 * core, 4 * half),
-            ),
-        ),
-    )
-    frame = key_block // BANDS % FRAMES
-    band = key_block % BANDS
-    cand = (offset * FRAMES + frame) * 3 + band - query_block % BANDS + 1
-    group = here + offset - REACH
-    exists = (group >= 0) & (group < tm_count)
-    hit = exists & (lax.broadcasted_iota(jnp.int32, shape, 2) == cand)
-    mine = (slot == OWN) & (key_block % BLOCKS == query_block)
-    hits = (hit & (block_list > 0)[None]) | mine
-    listed = jnp.max(hits.astype(jnp.float32), axis=2, keepdims=True)
-    listed = jnp.broadcast_to(listed, (SLOTS * BLOCKS, BLOCKS, BLOCK))
-    return jnp.where(listed > 0.5, 0.0, -jnp.inf).reshape(SLOTS * BLOCKS, TOK)
-
-
 def kernel(
     tm_count, heads,
-    q_ref, k_ref, v_ref, do_ref, bias_ref,
+    q_ref, k_ref, v_ref, do_ref, list_ref,
     dq_ref, dk_ref, dv_ref,
-    q_buf, do_buf, kv, back_out, back_in, own_acc, partner_acc, relay_acc,
-    row_sem, load_sem, fwd_send, fwd_recv, back_send, back_recv,
+    bias_ref, q_buf, do_buf, dq_buf, out_buf, kv, back_out, back_in, own_acc, partner_acc, relay_acc,
+    row_sem, load_sem, store_sem, fwd_send, fwd_recv, back_send, back_recv,
 ):
     here, core, half, down, up, has_relay, has_target = place(tm_count)
     sibling = here + 1 - 2 * core
@@ -119,6 +90,24 @@
     for row in rows:
         row.start()
 
+    offsets = (REACH, 3 - 2 * core, 4 - 4 * half, 1 + 2 * core, 4 * half)
+    query_block = lax.broadcasted_iota(jnp.int32, (1, TOK), 1) // BLOCK
+    for slot in range(SLOTS):
+        group = here + offsets[slot] - REACH
+        exists = ((group >= 0) & (group < tm_count)).astype(jnp.int32)
+        for key_block in range(BLOCKS):
+            frame, band = key_block // BANDS, key_block % BANDS
+            row = jnp.zeros((1, TOK), jnp.int32)
+            for at in range(BLOCKS):
+                if slot == OWN and at == key_block:
+                    listed = 1
+                else:
+                    cand = (offsets[slot] * FRAMES + frame) * 3 + band - at % BANDS + 1
+                    listed = list_ref[at, cand] * exists
+                row = jnp.where(query_block == at, listed, row)
+            index = slot * BLOCKS + key_block
+            bias_ref[index:index + 1, :] = jnp.where(row > 0, 0.0, -jnp.inf)
+
     @pl.when(~has_relay)
     def _():
         def clear(h, carry):
@@ -155,6 +144,12 @@
             recv_sem=back_recv.at[slot - 1, h],
             device_id={"tm": device},
             device_id_type=MESH,
+        )
+
+    def store(which, h):
+        src = dq_buf.at[h] if which == 0 else out_buf.at[h, pl.ds((which - 1) * TOK, TOK)]
+        return pltpu.make_async_copy(
+            src, (dq_ref, dk_ref, dv_ref)[which].at[:, columns(h)], store_sem.at[which, h]
         )
 
     def send_own(h):
@@ -250,7 +245,8 @@
                 acc = {OWN: own_acc, PARTNER: partner_acc, RELAY: relay_acc}[slot]
                 acc[h, 0:TOK, :] = key_part
                 acc[h, TOK:2 * TOK, :] = value_part
-        dq_ref[:, columns(h)] = (query_grad * scale).astype(jnp.bfloat16)
+        dq_buf[h] = (query_grad * scale).astype(jnp.bfloat16)
+        store(0, h).start()
 
         backward(SIB, h, sibling).start()
 
@@ -291,8 +287,9 @@
             + back_in[SIB - 1, h].astype(jnp.float32)
             + back_in[PARTNER - 1, h].astype(jnp.float32)
         ).astype(jnp.bfloat16)
-        dk_ref[:, columns(h)] = done[0:TOK]
-        dv_ref[:, columns(h)] = done[TOK:2 * TOK]
+        out_buf[h] = done
+        store(1, h).start()
+        store(2, h).start()
 
     stages = (
         (0, pass_partner), (1, pass_relay), (6, return_partner), (4, return_relay), (2, compute),
@@ -320,6 +317,8 @@
     lax.fori_loop(0, heads, last, 0)
 
     def drain(h, carry):
+        for which in range(3):
+            store(which, h).wait()
         forward(OWN, PARTNER, h, partner).wait_send()
         forward(OWN, SIB, h, sibling).wait_send()
         backward(SIB, h, sibling).wait_send()
@@ -346,20 +345,37 @@
     lax.fori_loop(0, heads, drain, 0)
 
 
+def settle_kernel(*refs):
+    sources, results, sems = refs[:3], refs[3:6], refs[6]
+    copies = [
+        pltpu.make_async_copy(
+            src.at[pl.ds(part * BLOCK, BLOCK)], dst.at[pl.ds(part * BLOCK, BLOCK)], sems.at[i, part]
+        )
+        for i, (src, dst) in enumerate(zip(sources, results))
+        for part in range(BLOCKS)
+    ]
+    for copy in copies:
+        copy.start()
+    for copy in copies:
+        copy.wait()
+
+
 def local(tm_count, queries, keys, values, grad_out, block_list):
     heads = queries.shape[1] // HDIM
-    bias = slot_bias(block_list, tm_count)
     out = jax.ShapeDtypeStruct(queries.shape, jnp.bfloat16)
-    vmem = pl.BlockSpec(memory_space=pltpu.VMEM)
+    hbm = pl.BlockSpec(memory_space=pl.ANY)
     pair = (heads, 2 * TOK, HDIM)
-    return pl.pallas_call(
+    grads = pl.pallas_call(
         functools.partial(kernel, tm_count, heads),
-        out_shape=(out, out, out),
-        in_specs=[pl.BlockSpec(memory_space=pl.ANY)] * 4 + [vmem],
-        out_specs=(vmem, vmem, vmem),
+        out_shape=(out,) * 3,
+        in_specs=[hbm] * 4 + [pl.BlockSpec(memory_space=pltpu.SMEM)],
+        out_specs=(hbm,) * 3,
         scratch_shapes=[
+            pltpu.VMEM((SLOTS * BLOCKS, TOK), jnp.float32),
             pltpu.VMEM(queries.shape, jnp.bfloat16),
             pltpu.VMEM(queries.shape, jnp.bfloat16),
+            pltpu.VMEM((heads, TOK, HDIM), jnp.bfloat16),
+            pltpu.VMEM(pair, jnp.bfloat16),
             pltpu.VMEM((SLOTS,) + pair, jnp.bfloat16),
             pltpu.VMEM((SLOTS - 1,) + pair, jnp.bfloat16),
             pltpu.VMEM((SLOTS - 1,) + pair, jnp.bfloat16),
@@ -368,6 +384,7 @@
             pltpu.VMEM(pair, jnp.float32),
             pltpu.SemaphoreType.DMA((2,)),
             pltpu.SemaphoreType.DMA((2, heads)),
+            pltpu.SemaphoreType.DMA((3, heads)),
             pltpu.SemaphoreType.DMA((SLOTS - 1, heads)),
             pltpu.SemaphoreType.DMA((SLOTS - 1, heads)),
             pltpu.SemaphoreType.DMA((SLOTS - 1, heads)),
@@ -376,7 +393,15 @@
         compiler_params=pltpu.CompilerParams(
             collective_id=0, has_side_effects=True, vmem_limit_bytes=56 * 2**20
         ),
-    )(queries, keys, values, grad_out, bias)
+    )(queries, keys, values, grad_out, block_list)
+    return pl.pallas_call(
+        settle_kernel,
+        out_shape=(out,) * 3,
+        in_specs=[hbm] * 3,
+        out_specs=(hbm,) * 3,
+        scratch_shapes=[pltpu.SemaphoreType.DMA((3, BLOCKS))],
+        compiler_params=pltpu.CompilerParams(vmem_limit_bytes=56 * 2**20),
+    )(*grads)
 
 
 def solution(mesh):

time: 84 us -> 150 us (1.79)
  Pallas kernels: 76.7 us -> 149 us
  local copies, waits for them, and re-layouts: 5.89 us -> 0 us
    pallas_call x0 -> x1, Pallas kernels: none -> 72.7 us  [local(): pl.pallas_call(settle_kernel, out_shape=(out,) * 3, in_specs=[hbm] * 3, o...]
    unnamed x9 -> x0, local copies, waits for them, and re-layouts: 5.11 us -> none
where the time goes in v4:
time: 150 us; the launch traced here: 149 us
  Pallas kernels  149 us (99%)
    pallas_call x1, Pallas kernels, local(): pl.pallas_call(functools.partial(kernel, tm_count, heads), out_shape=(out...  76.1 us
    pallas_call x1, Pallas kernels, local(): pl.pallas_call(settle_kernel, out_shape=(out,) * 3, in_specs=[hbm] * 3, o...  72.7 us

profile of v4, /device:TPU:0, one launch (start us, length us, event | category | flops | bytes accessed | tf_op | source)
XLA Modules:
  0.0 149.4 jit_solution(8103960793355371943)
XLA Ops:
  0.6 76.1 %shard_map.76 = (bf16[256,1536]{1,0:T(8,128)(2,1)}, bf16[256,1536]{1,0:T(8,128)(2,1)}, bf16[256,1536]{1,0:T(8,128)(2,1)}) custom-call(bf16[256,1536]{1,0:T(8,128)(2,1)} %q_ref.1, bf16[256,1536]{1,0:T(8,128)(2,1)} %k_ref.1, bf16[256,1536]{1,0:T(8,128)(2,1)} %v_ref.1, bf16[256,1536]{1,0:T(8,128)(2,1)} %do_ref.1, s32[4,30]{1,0:T(4,128)} %list_ref.1), custom_call_target="tpu_custom_call" | custom-call | tf_op jit(solution)/shard_map/pallas_call | solution.py:368
  76.7 72.7 %shard_map.77 = (bf16[256,1536]{1,0:T(8,128)(2,1)}, bf16[256,1536]{1,0:T(8,128)(2,1)}, bf16[256,1536]{1,0:T(8,128)(2,1)}) custom-call(bf16[256,1536]{1,0:T(8,128)(2,1)} %get-tuple-element.6.refs_0_, bf16[256,1536]{1,0:T(8,128)(2,1)} %get-tuple-element.7.refs_1_, bf16[256,1536]{1,0:T(8,128)(2,1)} %get-tuple-element.8.refs_2_), custom_call_target="tpu_custom_call" | custom-call | tf_op jit(solution)/shard_map/pallas_call | solution.py:397

commit v5 on v4

--- a/solution.py
+++ b/solution.py
@@ -346,18 +346,8 @@
 
 
 def settle_kernel(*refs):
-    sources, results, sems = refs[:3], refs[3:6], refs[6]
-    copies = [
-        pltpu.make_async_copy(
-            src.at[pl.ds(part * BLOCK, BLOCK)], dst.at[pl.ds(part * BLOCK, BLOCK)], sems.at[i, part]
-        )
-        for i, (src, dst) in enumerate(zip(sources, results))
-        for part in range(BLOCKS)
-    ]
-    for copy in copies:
-        copy.start()
-    for copy in copies:
-        copy.wait()
+    for src, dst in zip(refs[:3], refs[3:]):
+        dst[...] = src[...]
 
 
 def local(tm_count, queries, keys, values, grad_out, block_list):
@@ -394,12 +384,13 @@
             collective_id=0, has_side_effects=True, vmem_limit_bytes=56 * 2**20
         ),
     )(queries, keys, values, grad_out, block_list)
+    rows = pl.BlockSpec((BLOCK, queries.shape[1]), lambda i: (i, 0))
     return pl.pallas_call(
         settle_kernel,
         out_shape=(out,) * 3,
-        in_specs=[hbm] * 3,
-        out_specs=(hbm,) * 3,
-        scratch_shapes=[pltpu.SemaphoreType.DMA((3, BLOCKS))],
+        grid=(BLOCKS,),
+        in_specs=[rows] * 3,
+        out_specs=(rows,) * 3,
         compiler_params=pltpu.CompilerParams(vmem_limit_bytes=56 * 2**20),
     )(*grads)
 

time: 150 us -> 80.8 us (0.54)
  Pallas kernels: 149 us -> 80 us
    pallas_call x1, Pallas kernels: 72.7 us -> 3.91 us  [local(): pl.pallas_call(settle_kernel, out_shape=(out,) * 3, grid=(BLOCKS,), in_sp...]
where the time goes in v5:
time: 80.8 us; the launch traced here: 80.6 us
  Pallas kernels  80 us (99%)
    pallas_call x1, Pallas kernels, local(): pl.pallas_call(functools.partial(kernel, tm_count, heads), out_shape=(out...  76.1 us
    pallas_call x1, Pallas kernels, local(): pl.pallas_call(settle_kernel, out_shape=(out,) * 3, grid=(BLOCKS,), in_sp...  3.91 us

profile of v5, /device:TPU:0, one launch (start us, length us, event | category | flops | bytes accessed | tf_op | source)
XLA Modules:
  0.0 80.6 jit_solution(6887001341536288961)
XLA Ops:
  0.6 76.1 %shard_map.76 = (bf16[256,1536]{1,0:T(8,128)(2,1)}, bf16[256,1536]{1,0:T(8,128)(2,1)}, bf16[256,1536]{1,0:T(8,128)(2,1)}) custom-call(bf16[256,1536]{1,0:T(8,128)(2,1)} %q_ref.1, bf16[256,1536]{1,0:T(8,128)(2,1)} %k_ref.1, bf16[256,1536]{1,0:T(8,128)(2,1)} %v_ref.1, bf16[256,1536]{1,0:T(8,128)(2,1)} %do_ref.1, s32[4,30]{1,0:T(4,128)} %list_ref.1), custom_call_target="tpu_custom_call" | custom-call | tf_op jit(solution)/shard_map/pallas_call | solution.py:358
  76.7 3.9 %shard_map.77 = (bf16[256,1536]{1,0:T(8,128)(2,1)}, bf16[256,1536]{1,0:T(8,128)(2,1)}, bf16[256,1536]{1,0:T(8,128)(2,1)}) custom-call(bf16[256,1536]{1,0:T(8,128)(2,1)} %get-tuple-element.6.refs_0_, bf16[256,1536]{1,0:T(8,128)(2,1)} %get-tuple-element.7.refs_1_, bf16[256,1536]{1,0:T(8,128)(2,1)} %get-tuple-element.8.refs_2_), custom_call_target="tpu_custom_call" | custom-call | tf_op jit(solution)/shard_map/pallas_call | solution.py:388
